TPU v7x, 32 devices: a whole 2x2x4 slice. The times are simulated.
32 devices in a mesh: expert: 8 (over y, x, core), dp: 4 (over z).
Axes of the slice: x: 2, y: 2, z: 4, core: 2. Of those that a mesh axis runs over, the one named last changes fastest.
Arguments:
- tokens: bfloat16 [4096, 2048], P(('expert', 'dp')), may hold values from -6 to 6
- cotangent: bfloat16 [4096, 2048], P(('expert', 'dp')), may hold values from -6 to 6
- expert_ids: int32 [4096, 8], P(('expert', 'dp')), may hold values from 0 to 63, as said below
- gate_weights: float32 [4096, 8], P(('expert', 'dp')), may hold values from 0.05 to 1
- placement: int32 [8], replicated, may hold values from 0 to 7, as said below
- w_in: bfloat16 [8, 2048, 1536], P('expert'), may hold values from -0.125 to 0.125
- w_out: bfloat16 [8, 768, 2048], P('expert'), may hold values from -0.21875 to 0.21875
Outputs:
- mixed: bfloat16 [4096, 2048], P(('expert', 'dp'))
- x_grad: bfloat16 [4096, 2048], P(('expert', 'dp'))
- gate_grad: float32 [4096, 8], P(('expert', 'dp'))
- w_in_grad: bfloat16 [8, 2048, 1536], P('expert', 'dp')
- w_out_grad: bfloat16 [8, 768, 2048], P('expert', 'dp')
Inputs may be any that keep to these rules, and one draw needn't show every extreme that they name: `expert_ids`: each row names 8 different experts, at most two of them below 8. Among the 128 tokens of one device (an aligned block of rows, one data group every 4 blocks), no expert below 8 is named by more than 16 tokens, and in every data group one such expert is named by exactly 16 tokens of every device of the group. placement[i] is i or (i + 4) % 8, and placement[placement[i]] = i; at least one pair exchanges and at least one pair stays.
All inputs are finite; a program needn't handle non-finite values.
Results may differ from a plain program's by a relative error of at most 0.018.
Values may be sent and summed in bfloat16 or wider, within the bound.
A program may use at most 128 MiB of HBM per device.

v0:
```python
import jax
import jax.numpy as jnp
from jax import lax
from jax.sharding import PartitionSpec as P


def partner_2(block, axis, apart):
    count = lax.axis_size(axis)
    route = []
    for low in range(count):
        high = low | 1 << apart
        if high != low and high < count:
            route += [(low, high), (high, low)]
    return lax.ppermute(block, axis, route)


def shards(tokens, cotangent, expert_ids, gate_weights, placement, w_in, w_out):
    expert_count = lax.axis_size("expert")
    group_count = lax.axis_size("dp")
    own_index = lax.axis_index("expert")
    tok_rows = tokens.shape[0]
    model_width = tokens.shape[1]
    hidden_units = w_out.shape[1]
    pick_count = expert_ids.shape[1]
    capacity = tok_rows // 8
    slot_count = expert_count * capacity
    half_bit = expert_count.bit_length() - 2
    expert_lane = jnp.arange(expert_count, dtype=jnp.int32)
    partner = jnp.sum(jnp.where(expert_lane == own_index, placement, 0))
    is_moved = partner != own_index
    swapped = partner_2((w_in, w_out), "expert", half_bit)
    weight_in = jnp.where(is_moved, swapped[0], w_in)[0]
    weight_out = jnp.where(is_moved, swapped[1], w_out)[0]
    route_hot = (expert_ids.reshape(-1)[:, None] == expert_lane[None, :]).astype(jnp.int32)
    to_device = (placement[:, None] == expert_lane[None, :]).astype(jnp.int32)
    device_hot = jnp.dot(route_hot, to_device)
    slot_rank = jnp.cumsum(device_hot, axis=0) - device_hot
    slot_place = jnp.sum((slot_rank + expert_lane[None, :] * capacity) * device_hot, axis=1)
    is_live = jnp.sum(device_hot, axis=1) > 0
    slot_place = jnp.where(is_live, slot_place, -1).reshape(tok_rows, pick_count)
    slot_hot = slot_place[:, :, None] == jnp.arange(slot_count, dtype=jnp.int32)[None, None, :]
    select = jnp.sum(slot_hot.astype(jnp.bfloat16), axis=1)
    weigh = jnp.sum(jnp.where(slot_hot, gate_weights[:, :, None], 0.0), axis=1)
    slot_gate = jnp.sum(weigh, axis=0)
    send_x = jnp.einsum("ts,td->sd", select, tokens, preferred_element_type=jnp.float32).astype(
        jnp.bfloat16
    )
    send_dy = jnp.einsum("ts,td->sd", select, cotangent, preferred_element_type=jnp.float32)
    send_c = (send_dy * slot_gate[:, None]).astype(jnp.bfloat16)
    send_x = send_x.reshape(expert_count, capacity, model_width)
    send_c = send_c.reshape(expert_count, capacity, model_width)
    arrived_x = lax.all_to_all(send_x, "expert", split_axis=0, concat_axis=0, tiled=True)
    rows_x = arrived_x.reshape(slot_count, model_width)
    pre = jnp.dot(rows_x, weight_in, preferred_element_type=jnp.float32)
    gate_pre = pre[:, :hidden_units]
    up_pre = pre[:, hidden_units:]
    sigmoid_gate = jax.nn.sigmoid(gate_pre)
    activated = gate_pre * sigmoid_gate
    hidden = (activated * up_pre).astype(jnp.bfloat16)
    expert_out = jnp.dot(hidden, weight_out, preferred_element_type=jnp.float32).astype(
        jnp.bfloat16
    )
    returned = lax.all_to_all(
        expert_out.reshape(expert_count, capacity, model_width),
        "expert",
        split_axis=0,
        concat_axis=0,
        tiled=True,
    )
    returned = returned.reshape(slot_count, model_width)
    mixed = jnp.dot(
        weigh,
        returned.astype(jnp.float32),
        precision=lax.Precision.HIGHEST,
        preferred_element_type=jnp.float32,
    ).astype(jnp.bfloat16)
    scores = jnp.einsum("td,sd->ts", cotangent, returned, preferred_element_type=jnp.float32)
    gate_grad = jnp.sum(jnp.where(slot_hot, scores[:, None, :], 0.0), axis=2)
    arrived_c = lax.all_to_all(send_c, "expert", split_axis=0, concat_axis=0, tiled=True)
    rows_c = arrived_c.reshape(slot_count, model_width)
    hidden_grad = jnp.einsum("sd,fd->sf", rows_c, weight_out, preferred_element_type=jnp.float32)
    slope = sigmoid_gate * (1.0 + gate_pre * (1.0 - sigmoid_gate))
    gate_up_grad = jnp.concatenate(
        [hidden_grad * up_pre * slope, hidden_grad * activated], axis=1
    ).astype(jnp.bfloat16)
    pick_grad = jnp.einsum(
        "sf,df->sd", gate_up_grad, weight_in, preferred_element_type=jnp.float32
    ).astype(jnp.bfloat16)
    back = lax.all_to_all(
        pick_grad.reshape(expert_count, capacity, model_width),
        "expert",
        split_axis=0,
        concat_axis=0,
        tiled=True,
    )
    back = back.reshape(slot_count, model_width)
    x_grad = jnp.einsum("ts,sd->td", select, back, preferred_element_type=jnp.float32).astype(
        jnp.bfloat16
    )
    grad_in = (
        lax.psum_scatter(
            jnp.einsum(
                "sd,sf->df", rows_x, gate_up_grad, preferred_element_type=jnp.float32
            ).astype(jnp.bfloat16),
            "dp",
            scatter_dimension=0,
            tiled=True,
        ).astype(jnp.float32)
        / group_count
    ).astype(jnp.bfloat16)
    grad_out = (
        lax.psum_scatter(
            jnp.einsum("sf,sd->fd", hidden, rows_c, preferred_element_type=jnp.float32).astype(
                jnp.bfloat16
            ),
            "dp",
            scatter_dimension=0,
            tiled=True,
        ).astype(jnp.float32)
        / group_count
    ).astype(jnp.bfloat16)
    return (mixed, x_grad, gate_grad, grad_in[None], grad_out[None])


def solution(mesh):
    placed = (
        P(("expert", "dp"), None),
        P(("expert", "dp"), None),
        P(("expert", "dp"), None),
        P(("expert", "dp"), None),
        P(),
        P("expert", None, None),
        P("expert", None, None),
    )
    return jax.shard_map(
        shards,
        mesh=mesh,
        in_specs=placed,
        out_specs=(
            P(("expert", "dp"), None),
            P(("expert", "dp"), None),
            P(("expert", "dp"), None),
            P("expert", "dp", None),
            P("expert", "dp", None),
        ),
        check_vma=False,
    )
```

profile of v0, /device:TPU:0, one launch (start us, length us, event | category | flops | bytes accessed | tf_op | source)
XLA Modules:
  0.0 439.3 jit_solution(562757690274955059)
XLA Ops:
  7.2 3.0 collective-permute-start
  11.2 1.0 fusion.18
  12.2 2.3 reduce-window.6
  15.4 2.2 convolution_convert_fusion.4
  17.6 4.2 all-to-all-start
  21.7 1.3 fusion.27
  23.7 195.3 %all-to-all-done = bf16[8,16,2048]{2,1,0:T(8,128)(2,1)S(1)} async-done(((bf16[8,16,2048]{2,1,0:T(8,128)(2,1)}), bf16[8,16,2048]{2,1,0:T(8,128)(2,1)S(1)}, u32[]{:S(2)}, u32[]{:S(2)}) %all-to-all-start) | async-done | bytes 524320 | tf_op jit(solution)/shard_map/all_to_all | solution.py:52
  219.0 4.3 fusion.2
  223.4 3.5 fusion.9
  227.0 4.0 all-to-all-start.1
  231.1 9.6 %all-to-all-done.1 = bf16[8,16,2048]{2,1,0:T(8,128)(2,1)S(1)} async-done(((bf16[8,16,2048]{2,1,0:T(8,128)(2,1)}), bf16[8,16,2048]{2,1,0:T(8,128)(2,1)S(1)}, u32[]{:S(2)}, u32[]{:S(2)}) %all-to-all-start.1) | async-done | bytes 524320 | tf_op jit(solution)/shard_map/all_to_all | solution.py:63
  241.9 12.2 %all_to_all.20 = bf16[8,16,2048]{2,1,0:T(8,128)(2,1)S(1)} all-to-all(bf16[8,16,2048]{2,1,0:T(8,128)(2,1)S(1)} %bitcast.77), channel_id=1, replica_groups=mesh['expert'=8,'dp'=4] {'expert'}, dimensions={0} | all-to-all | bytes 1048576 | tf_op jit(solution)/shard_map/all_to_all | solution.py:79
  254.1 2.7 convolution_convert_fusion.1
  256.8 3.1 multiply_convert_fusion.3
  260.0 4.5 %convolution_convert_fusion = bf16[2048,1536]{1,0:T(8,128)(2,1)} fusion(bf16[128,2048]{1,0:T(8,128)(2,1)S(1)} %bitcast.75, bf16[128,768]{1,0:T(8,128)(2,1)S(1)} %get-tuple-element.16, bf16[128,768]{1,0:T(8,128)(2,1)S(1)} %get-tuple-element.15), kind=kOutput, calls=%fused_computation | convolution fusion | flops 809238528 | bytes 7208960 | tf_op jit(solution)/shard_map/sd,sf->df/dot_general | solution.py:102
  264.5 5.8 %fusion.12 = bf16[128,2048]{1,0:T(8,128)(2,1)} fusion(bf16[1,2048,1536]{2,1,0:T(8,128)(2,1)} %collective-permute-done, bf16[1,2048,1536]{2,1,0:T(8,128)(2,1)} %param.12, pred[]{:T(512)S(6)} %ne.3, bf16[128,768]{1,0:T(8,128)(2,1)S(1)} %get-tuple-element.16, bf16[128,768]{1,0:T(8,128)(2,1)S(1)} %get-tuple-element.15), kind=kOutput, calls=%fused_computation.19 | convolution fusion | flops 809500672 | bytes 13500417 | tf_op jit(solution)/shard_map/sf,df->sd/dot_general | solution.py:86
  270.2 3.5 all-to-all-start.3
  274.4 1.4 convolution_convert_fusion.3
  275.8 7.7 %all-to-all-done.3 = bf16[8,16,2048]{2,1,0:T(8,128)(2,1)S(1)} async-done(((bf16[8,16,2048]{2,1,0:T(8,128)(2,1)}), bf16[8,16,2048]{2,1,0:T(8,128)(2,1)S(1)}, u32[]{:S(2)}, u32[]{:S(2)}) %all-to-all-start.3) | async-done | bytes 524320 | tf_op jit(solution)/shard_map/all_to_all | solution.py:89
  283.4 1.1 convolution_convert_fusion.2
  284.5 32.1 %reduce-scatter.5.cloned.1.call-done = bf16[192,2048]{1,0:T(8,128)(2,1)} async-done(((bf16[768,2048]{1,0:T(8,128)(2,1)}), bf16[192,2048]{1,0:T(8,128)(2,1)}) %reduce-scatter.5.cloned.1.call-update) | async-done | bytes 786448 | tf_op jit(solution)/shard_map/reduce_scatter | solution.py:112
  316.6 2.2 fusion.16
  318.7 110.9 %reduce-scatter.3.cloned.1.call-done = bf16[512,1536]{1,0:T(8,128)(2,1)} async-done(((bf16[2048,1536]{1,0:T(8,128)(2,1)}), bf16[512,1536]{1,0:T(8,128)(2,1)}) %reduce-scatter.3.cloned.1.call-update) | async-done | bytes 1572880 | tf_op jit(solution)/shard_map/reduce_scatter | solution.py:101
  429.7 2.8 fusion.15
  (31 shorter events, 4.1 us)
Async XLA Ops:
  7.2 233.5 %copy-start = (bf16[128,2048]{1,0:T(8,128)(2,1)S(1)}, bf16[128,2048]{1,0:T(8,128)(2,1)}, u32[]{:S(2)}) copy-start(bf16[128,2048]{1,0:T(8,128)(2,1)} %param.8) | copy-start | bytes 1572868
  7.2 211.8 %collective-permute-start = (bf16[1,2048,1536]{2,1,0:T(8,128)(2,1)}, bf16[1,2048,1536]{2,1,0:T(8,128)(2,1)}, u32[]{:S(2)}, u32[]{:S(2)}) collective-permute-start(bf16[1,2048,1536]{2,1,0:T(8,128)(2,1)} %param.12), channel_id=1, source_target_pairs={{0,16},{16,0},{4,20},{20,4},{8,24},{24,8},{12,28},{28,12},{1,17},{... | collective-permute-start | bytes 18874376 | tf_op jit(solution)/shard_map/ppermute | solution.py:14
  10.2 213.2 %collective-permute-start.1 = (bf16[1,768,2048]{2,1,0:T(8,128)(2,1)}, bf16[1,768,2048]{2,1,0:T(8,128)(2,1)}, u32[]{:S(2)}, u32[]{:S(2)}) collective-permute-start(bf16[1,768,2048]{2,1,0:T(8,128)(2,1)} %param.13), channel_id=1, source_target_pairs={{0,16},{16,0},{4,20},{20,4},{8,24},{24,8},{12,28},{28,12},{1,17},{... | collective-permute-start | bytes 9437192 | tf_op jit(solution)/shard_map/ppermute | solution.py:14
  17.6 201.4 %all-to-all-start = ((bf16[8,16,2048]{2,1,0:T(8,128)(2,1)}), bf16[8,16,2048]{2,1,0:T(8,128)(2,1)S(1)}, u32[]{:S(2)}, u32[]{:S(2)}) async-start(bf16[8,16,2048]{2,1,0:T(8,128)(2,1)} %bitcast.3), calls=%async_computation | async-start | bytes 1048576 | tf_op jit(solution)/shard_map/all_to_all | solution.py:52
  219.0 4.5 %copy-start.2 = (bf16[1,768,2048]{2,1,0:T(8,128)(2,1)S(1)}, bf16[1,768,2048]{2,1,0:T(8,128)(2,1)}, u32[]{:S(2)}) copy-start(bf16[1,768,2048]{2,1,0:T(8,128)(2,1)} %param.13) | copy-start | bytes 9437188
  223.4 7.6 %copy-start.1 = (f32[128,8]{0,1:T(8,128)S(1)}, f32[128,8]{0,1:T(8,128)}, u32[]{:S(2)}) copy-start(f32[128,8]{0,1:T(8,128)} %param.10) | copy-start | bytes 12292
  227.0 13.7 %all-to-all-start.1 = ((bf16[8,16,2048]{2,1,0:T(8,128)(2,1)}), bf16[8,16,2048]{2,1,0:T(8,128)(2,1)S(1)}, u32[]{:S(2)}, u32[]{:S(2)}) async-start(bf16[8,16,2048]{2,1,0:T(8,128)(2,1)} %bitcast.7), calls=%async_computation.1 | async-start | bytes 1048576 | tf_op jit(solution)/shard_map/all_to_all | solution.py:63
  230.9 85.6 %reduce-scatter.5.cloned.1.call-start = ((), (), s32[]{:S(2)}) async-start(), calls=%async_computation.7 | async-start | bytes 3932160 | tf_op jit(solution)/shard_map/reduce_scatter | solution.py:112
  256.8 172.9 %reduce-scatter.3.cloned.1.call-start = ((), (), s32[]{:S(2)}) async-start(), calls=%async_computation.6 | async-start | bytes 7864320 | tf_op jit(solution)/shard_map/reduce_scatter | solution.py:101
  270.2 13.2 %all-to-all-start.3 = ((bf16[8,16,2048]{2,1,0:T(8,128)(2,1)}), bf16[8,16,2048]{2,1,0:T(8,128)(2,1)S(1)}, u32[]{:S(2)}, u32[]{:S(2)}) async-start(bf16[8,16,2048]{2,1,0:T(8,128)(2,1)} %bitcast.11), calls=%async_computation.3 | async-start | bytes 1048576 | tf_op jit(solution)/shard_map/all_to_all | solution.py:89
Sparse Core Ops, SparseCore 0:
  256.9 59.5 reduce-scatter.4
  318.9 110.7 reduce-scatter.2
where the time goes:
time: 439 us
  waiting for transfers between devices  356 us (81%)
  matrix products  30.1 us (7%)
  starting transfers between devices  14.8 us (3%)
  between operations  14.8 us (3%)
  blocking collectives  12.2 us (3%)
  other arithmetic  9.73 us (2%)
    all_to_all x1, waiting for transfers between devices, shards(): lax.all_to_all(send_x, 'expert', split_axis=0, concat_axis=0, tiled=True)  195 us
    reduce_scatter x1, waiting for transfers between devices, shards(): lax.psum_scatter(jnp.einsum('sd,sf->df', rows_x, gate_up_grad, preferred_...  111 us
    reduce_scatter x1, waiting for transfers between devices, shards(): lax.psum_scatter(jnp.einsum('sf,sd->fd', hidden, rows_c, preferred_elemen...  32.1 us
    all_to_all x1, blocking collectives, shards(): lax.all_to_all(send_c, 'expert', split_axis=0, concat_axis=0, tiled=True)  12.2 us
    all_to_all x1, waiting for transfers between devices, shards(): lax.all_to_all(expert_out.reshape(expert_count, capacity, model_width), '...  9.59 us
  transfers between devices with their start and end apart: 7, of which 5 were waited for; matrix products, arithmetic and copies ran while one was open for 7% of the time, Pallas kernels for 0%

commit v1 on v0

v1 whole, which is shorter than its diff:
```python
import jax
import jax.numpy as jnp
from jax import lax
from jax.sharding import PartitionSpec as P

F32 = jnp.float32
BF16 = jnp.bfloat16


def hidden_parts(rows_x, weight_in, hidden_units):
    pre = jnp.dot(rows_x, weight_in, preferred_element_type=F32)
    gate_pre = pre[:, :hidden_units]
    up_pre = pre[:, hidden_units:]
    sigmoid_gate = jax.nn.sigmoid(gate_pre)
    activated = gate_pre * sigmoid_gate
    hidden = (activated * up_pre).astype(BF16)
    slope = up_pre * sigmoid_gate * (1.0 + gate_pre * (1.0 - sigmoid_gate))
    return hidden, activated, slope


def pre_grad(rows_c, weight_out, activated, slope):
    hidden_grad = jnp.einsum("sd,fd->sf", rows_c, weight_out, preferred_element_type=F32)
    return jnp.concatenate([hidden_grad * slope, hidden_grad * activated], axis=1).astype(BF16)


def shards(tokens, cotangent, expert_ids, gate_weights, placement, w_in, w_out):
    expert_count = lax.axis_size("expert")
    group_count = lax.axis_size("dp")
    own_index = lax.axis_index("expert")
    group = lax.axis_index("dp")
    tok_rows, model_width = tokens.shape
    hidden_units = w_out.shape[1]
    capacity = tok_rows // 8
    slot_count = expert_count * capacity
    expert_lane = jnp.arange(expert_count, dtype=jnp.int32)
    placed_here = jnp.sum(jnp.where(expert_lane == own_index, placement, 0))
    is_moved = placed_here != own_index
    weight_in, weight_out = w_in[0], w_out[0]

    pick_hot = expert_ids[:, :, None] == expert_lane[None, None, :]
    expert_hot = jnp.any(pick_hot, axis=1)
    gate_of = jnp.sum(jnp.where(pick_hot, gate_weights[:, :, None], 0.0), axis=1)
    row = jnp.arange(tok_rows, dtype=jnp.int32)
    below = (row[None, :] < row[:, None]).astype(BF16)
    rank = jnp.dot(below, expert_hot.astype(BF16), preferred_element_type=F32).astype(jnp.int32)
    rank = jnp.where(expert_hot, rank, -1)
    slot_hot = rank[:, :, None] == jnp.arange(capacity, dtype=jnp.int32)[None, None, :]
    select = slot_hot.astype(BF16).reshape(tok_rows, slot_count)
    weigh = jnp.where(slot_hot, gate_of[:, :, None], 0.0).reshape(tok_rows, slot_count)
    slot_gate = jnp.sum(weigh, axis=0)

    send_x = jnp.einsum("ts,td->sd", select, tokens, preferred_element_type=F32).astype(BF16)
    send_dy = jnp.einsum("ts,td->sd", select, cotangent, preferred_element_type=F32)
    send_c = (send_dy * slot_gate[:, None]).astype(BF16)
    send = jnp.stack([send_x, send_c], axis=0).reshape(2, expert_count, capacity, model_width)
    arrived = lax.all_to_all(send, "expert", split_axis=1, concat_axis=1, tiled=True)
    arrived = arrived.reshape(2, slot_count, model_width)

    gathered = lax.all_gather(arrived, "dp", axis=1, tiled=True)

    hidden, activated, slope = hidden_parts(arrived[0], weight_in, hidden_units)
    expert_out = jnp.dot(hidden, weight_out, preferred_element_type=F32).astype(BF16)
    gate_up_grad = pre_grad(arrived[1], weight_out, activated, slope)
    pick_grad = jnp.einsum("sf,df->sd", gate_up_grad, weight_in, preferred_element_type=F32)
    back = jnp.stack([expert_out, pick_grad.astype(BF16)], axis=0)
    back = back.reshape(2, expert_count, capacity, model_width)
    back = lax.all_to_all(back, "expert", split_axis=1, concat_axis=1, tiled=True)
    back = back.reshape(2, slot_count, model_width)
    returned, back_grad = back[0], back[1]

    all_x, all_c = gathered[0], gathered[1]
    hidden, activated, slope = hidden_parts(all_x, weight_in, hidden_units)
    in_rows = model_width // group_count
    out_rows = hidden_units // group_count
    hidden_part = lax.dynamic_slice_in_dim(hidden, group * out_rows, out_rows, axis=1)
    grad_out = jnp.einsum("sf,sd->fd", hidden_part, all_c, preferred_element_type=F32)
    grad_out = (grad_out / group_count).astype(BF16)
    gate_up_grad = pre_grad(all_c, weight_out, activated, slope)
    x_part = lax.dynamic_slice_in_dim(all_x, group * in_rows, in_rows, axis=1)
    grad_in = jnp.einsum("sd,sf->df", x_part, gate_up_grad, preferred_element_type=F32)
    grad_in = (grad_in / group_count).astype(BF16)
    half = expert_count // 2
    route = [(i, (i + half) % expert_count) for i in range(expert_count)]
    swapped_out = lax.ppermute(grad_out, "expert", route)
    swapped_in = lax.ppermute(grad_in, "expert", route)

    weigh_high = weigh.astype(BF16)
    rest = weigh - weigh_high.astype(F32)
    weigh_mid = rest.astype(BF16)
    weigh_low = (rest - weigh_mid.astype(F32)).astype(BF16)
    mixed = jnp.dot(weigh_high, returned, preferred_element_type=F32)
    mixed += jnp.dot(weigh_mid, returned, preferred_element_type=F32)
    mixed += jnp.dot(weigh_low, returned, preferred_element_type=F32)
    scores = jnp.einsum("td,sd->ts", cotangent, returned, preferred_element_type=F32)
    scores = scores.reshape(tok_rows, expert_count, capacity)
    score_of = jnp.sum(jnp.where(slot_hot, scores, 0.0), axis=2)
    gate_grad = jnp.sum(jnp.where(pick_hot, score_of[:, None, :], 0.0), axis=2)
    x_grad = jnp.dot(select, back_grad, preferred_element_type=F32)
    grad_in = jnp.where(is_moved, swapped_in, grad_in)
    grad_out = jnp.where(is_moved, swapped_out, grad_out)
    return (mixed.astype(BF16), x_grad.astype(BF16), gate_grad, grad_in[None], grad_out[None])


def solution(mesh):
    rows = P(("expert", "dp"), None)
    weights = P("expert", None, None)
    grads = P("expert", "dp", None)
    return jax.shard_map(
        shards,
        mesh=mesh,
        in_specs=(rows, rows, rows, rows, P(), weights, weights),
        out_specs=(rows, rows, rows, grads, grads),
        check_vma=False,
    )
```

time: 439 us -> 189 us (0.43)
  waiting for transfers between devices: 356 us -> 107 us
  starting transfers between devices: 14.8 us -> 6.43 us
  blocking collectives: 12.2 us -> 20.3 us
  local copies, waits for them, and re-layouts: 2.12 us -> 7.99 us
  matrix products: 30.1 us -> 25.1 us
    all_to_all x3 -> x1, waiting for transfers between devices: 213 us -> 14.1 us  [shards(): lax.all_to_all(back, 'expert', split_axis=1, concat_axis=1, tiled=True)]
    reduce_scatter x2 -> x0, waiting for transfers between devices: 143 us -> none  [the longest x1 111 us: shards(): lax.psum_scatter(jnp.einsum('sd,sf->df', rows_x, gate_up_grad, preferred_...]
    ppermute x2, waiting for transfers between devices: 0.01 us -> 47.5 us  [the longest x1 47.5 us: shards(): swapped_out = lax.ppermute(grad_out, 'expert', route)]
    all_gather x0 -> x1, waiting for transfers between devices: none -> 45.7 us  [shards(): gathered = lax.all_gather(arrived, 'dp', axis=1, tiled=True)]
    all_to_all x1, blocking collectives: 12.2 us -> 20.3 us  [shards(): lax.all_to_all(send, 'expert', split_axis=1, concat_axis=1, tiled=True)]
    all_to_all x3 -> x1, starting transfers between devices: 11.6 us -> 4.24 us  [shards(): lax.all_to_all(back, 'expert', split_axis=1, concat_axis=1, tiled=True)]
    dot_general x12 -> x16, matrix products: 30.1 us -> 25.1 us  [the longest x2 10.1 us: hidden_parts(): pre = jnp.dot(rows_x, weight_in, preferred_element_type=F32)]
  transfers between devices with their start and end apart: 7 -> 4, of which waited for: 5 -> 3; matrix products, arithmetic and copies ran while one was open for 7% -> 10% of each run, Pallas kernels for 0% -> 0%
where the time goes in v1:
time: 189 us
  waiting for transfers between devices  107 us (57%)
  matrix products  25.1 us (13%)
  blocking collectives  20.3 us (11%)
  between operations  14.9 us (8%)
  local copies, waits for them, and re-layouts  7.99 us (4%)
  other arithmetic  6.48 us (3%)
  starting transfers between devices  6.43 us (3%)
    ppermute x1, waiting for transfers between devices, shards(): swapped_out = lax.ppermute(grad_out, 'expert', route)  47.5 us
    all_gather x1, waiting for transfers between devices, shards(): gathered = lax.all_gather(arrived, 'dp', axis=1, tiled=True)  45.7 us
    all_to_all x1, blocking collectives, shards(): lax.all_to_all(send, 'expert', split_axis=1, concat_axis=1, tiled=True)  20.3 us
    all_to_all x1, waiting for transfers between devices, shards(): lax.all_to_all(back, 'expert', split_axis=1, concat_axis=1, tiled=True)  14.1 us
    dot_general x2, matrix products, hidden_parts(): pre = jnp.dot(rows_x, weight_in, preferred_element_type=F32)  10.1 us
    all_to_all x1, starting transfers between devices, shards(): lax.all_to_all(back, 'expert', split_axis=1, concat_axis=1, tiled=True)  4.24 us
  transfers between devices with their start and end apart: 4, of which 3 were waited for; matrix products, arithmetic and copies ran while one was open for 10% of the time, Pallas kernels for 0%

profile of v1, /device:TPU:0, one launch (start us, length us, event | category | flops | bytes accessed | tf_op | source)
XLA Modules:
  0.0 188.6 jit_solution(10954590810563749613)
XLA Ops:
  9.3 1.3 convolution_convert_fusion.1
  10.7 1.3 fusion.14
  12.1 20.3 %all_to_all.10 = bf16[2,8,16,2048]{3,2,0,1:T(8,128)(2,1)S(1)} all-to-all(bf16[2,8,16,2048]{3,2,0,1:T(8,128)(2,1)S(1)} %pad_maximum_fusion), channel_id=1, replica_groups=mesh['expert'=8,'dp'=4] {'expert'}, dimensions={1} | all-to-all | bytes 2097152 | tf_op jit(solution)/shard_map/all_to_all | solution.py:56
  32.4 1.0 copy-done.3
  33.4 1.0 copy.33
  34.5 1.4 fusion.47
  35.9 3.9 %fusion.4 = f32[128,1536]{1,0:T(8,128)S(1)} fusion(bf16[128,2048]{1,0:T(8,128)(2,1)S(1)} %bitcast.88, bf16[1,2048,1536]{2,1,0:T(8,128)(2,1)} %param.12), kind=kOutput, calls=%fused_computation.4 | convolution fusion | flops 805306368 | bytes 7602176 | tf_op jit(solution)/shard_map/dot_general | solution.py:11
  40.5 1.2 multiply_convert_fusion.3
  41.8 2.2 %fusion.19 = bf16[128,2048]{1,0:T(8,128)(2,1)S(1)} fusion(bf16[1,2048,1536]{2,1,0:T(8,128)(2,1)S(1)} %bitcast.83, bf16[128,768]{1,0:T(8,128)(2,1)S(1)} %get-tuple-element.10, bf16[128,768]{1,0:T(8,128)(2,1)S(1)} %get-tuple-element.9), kind=kOutput, calls=%fused_computation.24 | convolution fusion | flops 806354944 | bytes 7208960 | tf_op jit(solution)/shard_map/sf,df->sd/dot_general | solution.py:64
  43.9 1.1 pad_maximum_fusion.1
  45.0 4.2 %all-to-all-start.1 = ((bf16[2,8,16,2048]{3,2,0,1:T(8,128)(2,1)}), bf16[2,8,16,2048]{3,2,0,1:T(8,128)(2,1)}, u32[]{:S(2)}, u32[]{:S(2)}) async-start(bf16[2,8,16,2048]{3,2,0,1:T(8,128)(2,1)} %pad_maximum_fusion.1), calls=%async_computation.1 | async-start | bytes 2097152 | tf_op jit(solution)/shard_map/all_to_all | solution.py:67
  50.6 14.1 %all-to-all-done.1 = bf16[2,8,16,2048]{3,2,0,1:T(8,128)(2,1)} async-done(((bf16[2,8,16,2048]{3,2,0,1:T(8,128)(2,1)}), bf16[2,8,16,2048]{3,2,0,1:T(8,128)(2,1)}, u32[]{:S(2)}, u32[]{:S(2)}) %all-to-all-start.1) | async-done | bytes 1048608 | tf_op jit(solution)/shard_map/all_to_all | solution.py:67
  64.7 2.2 %fusion.46 = (bf16[1,8,16,2048]{3,2,0,1:T(8,128)(2,1)}, bf16[1,8,16,2048]{3,2,0,1:T(8,128)(2,1)S(1)}) fusion(bf16[2,8,16,2048]{3,2,0,1:T(8,128)(2,1)} %all-to-all-done.1), kind=kLoop, calls=%fused_computation.73 | loop fusion | bytes 2097152 | tf_op jit(solution)/shard_map/slice | solution.py:69
  67.8 1.3 fusion.50
  69.0 45.7 %all-gather.2.cloned.1.call-done = bf16[2,512,2048]{2,1,0:T(8,128)(2,1)} async-done(((bf16[2,128,2048]{2,1,0:T(8,128)(2,1)}), bf16[2,512,2048]{2,1,0:T(8,128)(2,1)}) %all-gather.2.cloned.1.call-update) | async-done | bytes 4194320 | tf_op jit(solution)/shard_map/all_gather | solution.py:59
  114.7 6.2 %fusion = f32[512,1536]{1,0:T(8,128)S(1)} fusion(bf16[1,2048,1536]{2,1,0:T(8,128)(2,1)} %param.12, bf16[2,512,2048]{2,1,0:T(8,128)(2,1)} %all-gather.2.cloned.1.call-done), kind=kOutput, calls=%fused_computation | convolution fusion | flops 3221225472 | bytes 11534336 | tf_op jit(solution)/shard_map/dot_general | solution.py:11
  120.9 2.2 %copy-done.5 = bf16[2,512,2048]{2,1,0:T(8,128)(2,1)S(1)} copy-done((bf16[2,512,2048]{2,1,0:T(8,128)(2,1)S(1)}, bf16[2,512,2048]{2,1,0:T(8,128)(2,1)}, u32[]{:S(2)}) %copy-start.5) | copy-done | bytes 4194328
  123.1 2.3 %multiply_convert_fusion.1 = (bf16[512,768]{1,0:T(8,128)(2,1)S(1)}, bf16[512,768]{1,0:T(8,128)(2,1)S(1)}, f32[512,768]{1,0:T(8,128)S(1)}, f32[512,768]{1,0:T(8,128)S(1)}) fusion(f32[512,1536]{1,0:T(8,128)S(1)} %fusion, bf16[1,768,2048]{2,1,0:T(8,128)(2,1)S(1)} %copy-done, bf16[2,512,2048]{2,1,0:T(8,128)(2,1)S(1)} %copy-done.5), kind=kOutput, calls=%fused_computation.32 | convolution fusion | flops 1615724544 | bytes 13107200 | tf_op jit(solution)/shard_map/sd,fd->sf/dot_general | solution.py:22
  125.4 1.0 fusion.12
  126.4 1.6 collective-permute-start
  129.4 1.1 convolution_convert_fusion
  130.8 1.1 fusion.15
  131.9 47.5 %collective-permute-done.1 = bf16[192,2048]{1,0:T(8,128)(2,1)S(1)} collective-permute-done((bf16[192,2048]{1,0:T(8,128)(2,1)S(1)}, bf16[192,2048]{1,0:T(8,128)(2,1)S(1)}, u32[]{:S(2)}, u32[]{:S(2)}) %collective-permute-start.1) | collective-permute-done | bytes 786464 | tf_op jit(solution)/shard_map/ppermute | solution.py:84
  180.4 1.3 select_bitcast_fusion
  (47 shorter events, 7.2 us)
Async XLA Ops:
  7.2 32.7 %copy-start = (bf16[1,768,2048]{2,1,0:T(8,128)(2,1)S(1)}, bf16[1,768,2048]{2,1,0:T(8,128)(2,1)}, u32[]{:S(2)}) copy-start(bf16[1,768,2048]{2,1,0:T(8,128)(2,1)} %param.13) | copy-start | bytes 9437188
  7.2 107.6 %all-gather.2.cloned.1.call-start = ((), (), s32[]{:S(2)}) async-start(), calls=%async_computation.2 | async-start | bytes 5242880 | tf_op jit(solution)/shard_map/all_gather | solution.py:59
  32.4 1.0 copy-start.3
  34.5 7.3 %slice-start = ((s8[6291456]{0:T(1024)(128)(4,1)}), s8[4194304]{0:T(1024)(128)(4,1)S(1)}, s32[]{:S(2)}) async-start(s8[6291456]{0:T(1024)(128)(4,1)} %bitcast.82), calls=%async_computation.3 | async-start | bytes 8388608
  35.9 5.8 %slice-start.1 = ((s8[6291456]{0:T(1024)(128)(4,1)}), s8[2097152]{0:T(1024)(128)(4,1)S(1)}, s32[]{:S(2)}) async-start(s8[6291456]{0:T(1024)(128)(4,1)} %bitcast.82), calls=%async_computation.4 | async-start | bytes 4194304
  43.9 5.3 %copy-start.9 = (s32[8]{0:T(128)S(1)}, s32[8]{0:T(128)}, u32[]{:S(2)}) copy-start(s32[8]{0:T(128)} %param.11) | copy-start | bytes 100
  45.0 19.7 %all-to-all-start.1 = ((bf16[2,8,16,2048]{3,2,0,1:T(8,128)(2,1)}), bf16[2,8,16,2048]{3,2,0,1:T(8,128)(2,1)}, u32[]{:S(2)}, u32[]{:S(2)}) async-start(bf16[2,8,16,2048]{3,2,0,1:T(8,128)(2,1)} %pad_maximum_fusion.1), calls=%async_computation.1 | async-start | bytes 2097152 | tf_op jit(solution)/shard_map/all_to_all | solution.py:67
  49.2 17.9 %copy-start.8 = (s32[128,8]{0,1:T(8,128)S(1)}, s32[128,8]{0,1:T(8,128)}, u32[]{:S(2)}) copy-start(s32[128,8]{0,1:T(8,128)} %param.9) | copy-start | bytes 12292
  64.7 2.2 %copy-start.6 = (bf16[128,2048]{1,0:T(8,128)(2,1)S(1)}, bf16[128,2048]{1,0:T(8,128)(2,1)}, u32[]{:S(2)}) copy-start(bf16[128,2048]{1,0:T(8,128)(2,1)} %param.8) | copy-start | bytes 1572868
  66.8 0.9 copy-start.1
  120.9 2.2 %copy-start.5 = (bf16[2,512,2048]{2,1,0:T(8,128)(2,1)S(1)}, bf16[2,512,2048]{2,1,0:T(8,128)(2,1)}, u32[]{:S(2)}) copy-start(bf16[2,512,2048]{2,1,0:T(8,128)(2,1)} %all-gather.2.cloned.1.call-done) | copy-start | bytes 12582916
  123.1 2.3 %slice-start.2 = ((bf16[2,512,2048]{2,1,0:T(8,128)(2,1)}), bf16[1,512,2048]{2,1,0:T(8,128)(2,1)S(1)}, s32[]{:S(2)}) async-start(bf16[2,512,2048]{2,1,0:T(8,128)(2,1)} %all-gather.2.cloned.1.call-done), calls=%async_computation.5 | async-start | bytes 4194304 | tf_op jit(solution)/shard_map/slice | solution.py:71
  126.4 54.0 %collective-permute-start = (bf16[512,1536]{1,0:T(8,128)(2,1)S(1)}, bf16[512,1536]{1,0:T(8,128)(2,1)S(1)}, u32[]{:S(2)}, u32[]{:S(2)}) collective-permute-start(bf16[512,1536]{1,0:T(8,128)(2,1)S(1)} %fusion.12), channel_id=1, source_target_pairs={{0,16},{4,20},{8,24},{12,28},{16,0},{20,4},{24,8},{28,12},{1,17},{... | collective-permute-start | bytes 4718600 | tf_op jit(solution)/shard_map/ppermute | solution.py:85
  128.0 1.4 copy-start.7
  128.0 2.5 %copy-start.2 = (bf16[1,8,16,2048]{3,2,0,1:T(8,128)(2,1)S(1)}, bf16[1,8,16,2048]{3,2,0,1:T(8,128)(2,1)}, u32[]{:S(2)}) copy-start(bf16[1,8,16,2048]{3,2,0,1:T(8,128)(2,1)} %copy-done.1) | copy-start | bytes 1572868
  128.0 2.5 %copy-start.4 = (f32[128,2048]{1,0:T(8,128)S(1)}, f32[128,2048]{1,0:T(8,128)}, u32[]{:S(2)}) copy-start(f32[128,2048]{1,0:T(8,128)} %fusion.50) | copy-start | bytes 3145732
  128.8 50.7 %collective-permute-start.1 = (bf16[192,2048]{1,0:T(8,128)(2,1)S(1)}, bf16[192,2048]{1,0:T(8,128)(2,1)S(1)}, u32[]{:S(2)}, u32[]{:S(2)}) collective-permute-start(bf16[192,2048]{1,0:T(8,128)(2,1)S(1)} %fusion.13), channel_id=1, source_target_pairs={{0,16},{4,20},{8,24},{12,28},{16,0},{20,4},{24,8},{28,12},{1,17},{... | collective-permute-start | bytes 2359304 | tf_op jit(solution)/shard_map/ppermute | solution.py:84
Sparse Core Ops, SparseCore 0:
  34.6 80.1 all-gather.1

commit v2 on v1

--- a/solution.py
+++ b/solution.py
@@ -21,6 +21,20 @@
 def pre_grad(rows_c, weight_out, activated, slope):
     hidden_grad = jnp.einsum("sd,fd->sf", rows_c, weight_out, preferred_element_type=F32)
     return jnp.concatenate([hidden_grad * slope, hidden_grad * activated], axis=1).astype(BF16)
+
+
+def exchange_columns(block, group, group_count):
+    rows, width = block.shape
+    part = width // group_count
+    whole = jnp.zeros((group_count, rows, part), block.dtype)
+    for shift in range(group_count):
+        target = (group + shift) % group_count
+        source = (group + group_count - shift) % group_count
+        piece = lax.dynamic_slice_in_dim(block, target * part, part, axis=1)
+        if shift:
+            piece = lax.ppermute(piece, "dp", [(i, (i + shift) % group_count) for i in range(group_count)])
+        whole = lax.dynamic_update_index_in_dim(whole, piece, source, axis=0)
+    return whole.reshape(group_count * rows, part)
 
 
 def shards(tokens, cotangent, expert_ids, gate_weights, placement, w_in, w_out):
@@ -56,11 +70,12 @@
     arrived = lax.all_to_all(send, "expert", split_axis=1, concat_axis=1, tiled=True)
     arrived = arrived.reshape(2, slot_count, model_width)
 
-    gathered = lax.all_gather(arrived, "dp", axis=1, tiled=True)
-
     hidden, activated, slope = hidden_parts(arrived[0], weight_in, hidden_units)
+    gate_up_grad = pre_grad(arrived[1], weight_out, activated, slope)
+    x_slices = exchange_columns(arrived[0], group, group_count)
+    all_grad = lax.all_gather(gate_up_grad, "dp", axis=0, tiled=True)
+    hidden_slices = exchange_columns(hidden, group, group_count)
     expert_out = jnp.dot(hidden, weight_out, preferred_element_type=F32).astype(BF16)
-    gate_up_grad = pre_grad(arrived[1], weight_out, activated, slope)
     pick_grad = jnp.einsum("sf,df->sd", gate_up_grad, weight_in, preferred_element_type=F32)
     back = jnp.stack([expert_out, pick_grad.astype(BF16)], axis=0)
     back = back.reshape(2, expert_count, capacity, model_width)
@@ -68,21 +83,16 @@
     back = back.reshape(2, slot_count, model_width)
     returned, back_grad = back[0], back[1]
 
-    all_x, all_c = gathered[0], gathered[1]
-    hidden, activated, slope = hidden_parts(all_x, weight_in, hidden_units)
-    in_rows = model_width // group_count
-    out_rows = hidden_units // group_count
-    hidden_part = lax.dynamic_slice_in_dim(hidden, group * out_rows, out_rows, axis=1)
-    grad_out = jnp.einsum("sf,sd->fd", hidden_part, all_c, preferred_element_type=F32)
-    grad_out = (grad_out / group_count).astype(BF16)
-    gate_up_grad = pre_grad(all_c, weight_out, activated, slope)
-    x_part = lax.dynamic_slice_in_dim(all_x, group * in_rows, in_rows, axis=1)
-    grad_in = jnp.einsum("sd,sf->df", x_part, gate_up_grad, preferred_element_type=F32)
-    grad_in = (grad_in / group_count).astype(BF16)
     half = expert_count // 2
     route = [(i, (i + half) % expert_count) for i in range(expert_count)]
+    own_c, all_grad = lax.optimization_barrier((arrived[1], all_grad))
+    all_c = lax.all_gather(own_c, "dp", axis=0, tiled=True)
+    grad_in = jnp.einsum("sd,sf->df", x_slices, all_grad, preferred_element_type=F32)
+    grad_in = (grad_in / group_count).astype(BF16)
+    swapped_in = lax.ppermute(grad_in, "expert", route)
+    grad_out = jnp.einsum("sf,sd->fd", hidden_slices, all_c, preferred_element_type=F32)
+    grad_out = (grad_out / group_count).astype(BF16)
     swapped_out = lax.ppermute(grad_out, "expert", route)
-    swapped_in = lax.ppermute(grad_in, "expert", route)
 
     weigh_high = weigh.astype(BF16)
     rest = weigh - weigh_high.astype(F32)

time: 189 us -> 166 us (0.88)
  waiting for transfers between devices: 107 us -> 69.1 us
  starting transfers between devices: 6.43 us -> 14 us
  local copies, waits for them, and re-layouts: 7.99 us -> 15.4 us
  matrix products: 25.1 us -> 20.5 us
  other arithmetic: 6.48 us -> 10.4 us
    ppermute x1, waiting for transfers between devices: 47.5 us -> 13 us  [shards(): swapped_out = lax.ppermute(grad_out, 'expert', route)]
    all_to_all x1, waiting for transfers between devices: 14.1 us -> 0.01 us  [shards(): lax.all_to_all(back, 'expert', split_axis=1, concat_axis=1, tiled=True)]
    dot_general x2 -> x1, matrix products: 10.1 us -> 1.9 us  [hidden_parts(): pre = jnp.dot(rows_x, weight_in, preferred_element_type=F32)]
    dynamic_update_slice x0 -> x8, local copies, waits for them, and re-layouts: none -> 8.04 us  [exchange_columns(): whole = lax.dynamic_update_index_in_dim(whole, piece, source, axis=0)]
    ppermute x0 -> x6, starting transfers between devices: none -> 7.44 us  [exchange_columns(): lax.ppermute(piece, 'dp', [(i, (i + shift) % group_count) for i in range(...]
    all_gather x1 -> x2, waiting for transfers between devices: 45.7 us -> 51.2 us  [the longest x1 27.3 us: shards(): all_c = lax.all_gather(own_c, 'dp', axis=0, tiled=True)]
    ppermute x0 -> x6, waiting for transfers between devices: none -> 4.9 us  [exchange_columns(): lax.ppermute(piece, 'dp', [(i, (i + shift) % group_count) for i in range(...]
    dot_general x1, matrix products: 2.15 us -> 4.92 us  [shards(): jnp.einsum('sf,df->sd', gate_up_grad, weight_in, preferred_element_type=F32)]
  transfers between devices with their start and end apart: 4 -> 11, of which waited for: 3 -> 4; matrix products, arithmetic and copies ran while one was open for 10% -> 20% of each run, Pallas kernels for 0% -> 0%
where the time goes in v2:
time: 166 us; the launch traced here: 165 us
  waiting for transfers between devices  69.1 us (42%)
  blocking collectives  20.6 us (12%)
  matrix products  20.5 us (12%)
  local copies, waits for them, and re-layouts  15.4 us (9%)
  between operations  15.1 us (9%)
  starting transfers between devices  14 us (8%)
  other arithmetic  10.4 us (6%)
    all_gather x1, waiting for transfers between devices, shards(): all_c = lax.all_gather(own_c, 'dp', axis=0, tiled=True)  27.3 us
    all_gather x1, waiting for transfers between devices, shards(): all_grad = lax.all_gather(gate_up_grad, 'dp', axis=0, tiled=True)  23.9 us
    all_to_all x1, blocking collectives, shards(): lax.all_to_all(send, 'expert', split_axis=1, concat_axis=1, tiled=True)  20.6 us
    ppermute x1, waiting for transfers between devices, shards(): swapped_out = lax.ppermute(grad_out, 'expert', route)  13 us
    dynamic_update_slice x8, local copies, waits for them, and re-layouts, exchange_columns(): whole = lax.dynamic_update_index_in_dim(whole, piece, source, axis=0)  8.04 us
    ppermute x6, starting transfers between devices, exchange_columns(): lax.ppermute(piece, 'dp', [(i, (i + shift) % group_count) for i in range(...  7.44 us
    dot_general x1, matrix products, shards(): jnp.einsum('sf,df->sd', gate_up_grad, weight_in, preferred_element_type=F32)  4.92 us
    ppermute x6, waiting for transfers between devices, exchange_columns(): lax.ppermute(piece, 'dp', [(i, (i + shift) % group_count) for i in range(...  4.9 us
  transfers between devices with their start and end apart: 11, of which 4 were waited for; matrix products, arithmetic and copies ran while one was open for 20% of the time, Pallas kernels for 0%

profile of v2, /device:TPU:0, one launch (start us, length us, event | category | flops | bytes accessed | tf_op | source)
XLA Modules:
  0.0 165.1 jit_solution(15319357344129816397)
XLA Ops:
  9.9 1.3 convolution_convert_fusion.1
  11.2 1.3 fusion.10
  12.7 20.6 %all_to_all.10 = bf16[2,8,16,2048]{3,2,0,1:T(8,128)(2,1)S(1)} all-to-all(bf16[2,8,16,2048]{3,2,0,1:T(8,128)(2,1)S(1)} %pad_maximum_fusion), channel_id=1, replica_groups=mesh['expert'=8,'dp'=4] {'expert'}, dimensions={1} | all-to-all | bytes 2097152 | tf_op jit(solution)/shard_map/all_to_all | solution.py:70
  34.1 1.9 %fusion.2 = f32[128,1536]{1,0:T(8,128)} fusion(bf16[128,2048]{1,0:T(8,128)(2,1)S(1)} %bitcast.90, bf16[1,2048,1536]{2,1,0:T(8,128)(2,1)S(1)} %copy-done.1), kind=kOutput, calls=%fused_computation.2 | convolution fusion | flops 805306368 | bytes 7602176 | tf_op jit(solution)/shard_map/dot_general | solution.py:11
  36.0 2.5 %multiply_convert_fusion.1 = (bf16[128,768]{1,0:T(8,128)(2,1)S(1)}, bf16[128,768]{1,0:T(8,128)(2,1)S(1)}, bf16[128,768]{1,0:T(8,128)(2,1)S(1)}) fusion(f32[128,1536]{1,0:T(8,128)} %fusion.2, bf16[128,2048]{1,0:T(8,128)(2,1)} %bitcast.94, bf16[1,768,2048]{2,1,0:T(8,128)(2,1)S(1)} %copy-done), kind=kOutput, calls=%fused_computation.29 | convolution fusion | flops 404127744 | bytes 5046272 | tf_op jit(solution)/shard_map/sd,fd->sf/dot_general | solution.py:22
  42.7 1.8 %constant_dynamic-slice_fusion.3 = (bf16[128,512]{1,0:T(8,128)(2,1)}, bf16[128,512]{1,0:T(8,128)(2,1)}, bf16[128,512]{1,0:T(8,128)(2,1)}) fusion(bf16[128,2048]{1,0:T(8,128)(2,1)} %bitcast.91, s32[]{:T(128)S(6)} %select_n.168, s32[]{:T(128)S(6)} %select_n.166, s32[]{:T(128)S(6)} %select_n.162), kind=kLoop, calls=%fused_computation.57 | loop fusion | bytes 786444 | tf_op jit(solution)/shard_map/dynamic_slice | solution.py:33
  44.5 3.6 %collective-permute-start.2 = (bf16[128,512]{1,0:T(8,128)(2,1)}, bf16[128,512]{1,0:T(8,128)(2,1)}, u32[]{:S(2)}, u32[]{:S(2)}) collective-permute-start(bf16[128,512]{1,0:T(8,128)(2,1)} %get-tuple-element.16), channel_id=1, source_target_pairs={{0,3},{1,0},{2,1},{3,2},{4,7},{5,4},{6,5},{7,6},{8,11},{9,8},{10,9... | collective-permute-start | bytes 393224 | tf_op jit(solution)/shard_map/ppermute | solution.py:35
  49.9 2.8 %collective-permute-start.6 = (bf16[128,192]{1,0:T(8,128)(2,1)}, bf16[128,192]{1,0:T(8,128)(2,1)}, u32[]{:S(2)}, u32[]{:S(2)}) collective-permute-start(bf16[128,192]{1,0:T(8,128)(2,1)} %get-tuple-element.19), channel_id=1, source_target_pairs={{0,3},{1,0},{2,1},{3,2},{4,7},{5,4},{6,5},{7,6},{8,11},{9,8},{10,9... | collective-permute-start | bytes 147464 | tf_op jit(solution)/shard_map/ppermute | solution.py:35
  53.4 4.9 %fusion.15 = bf16[128,2048]{1,0:T(8,128)(2,1)S(1)} fusion(bf16[1,2048,1536]{2,1,0:T(8,128)(2,1)} %param.12, bf16[128,768]{1,0:T(8,128)(2,1)S(1)} %copy-done.8, bf16[128,768]{1,0:T(8,128)(2,1)S(1)} %get-tuple-element.9), kind=kOutput, calls=%fused_computation.20 | convolution fusion | flops 806354944 | bytes 7208960 | tf_op jit(solution)/shard_map/sf,df->sd/dot_general | solution.py:79
  58.3 1.1 pad_maximum_fusion.1
  59.4 4.4 %all-to-all-start.1 = ((bf16[2,8,16,2048]{3,2,0,1:T(8,128)(2,1)}), bf16[2,8,16,2048]{3,2,0,1:T(8,128)(2,1)}, u32[]{:S(2)}, u32[]{:S(2)}) async-start(bf16[2,8,16,2048]{3,2,0,1:T(8,128)(2,1)} %pad_maximum_fusion.1), calls=%async_computation.1 | async-start | bytes 2097152 | tf_op jit(solution)/shard_map/all_to_all | solution.py:82
  63.8 23.9 %all-gather.3.cloned.1.call-done = bf16[512,1536]{1,0:T(8,128)(2,1)} async-done(((bf16[128,1536]{1,0:T(8,128)(2,1)}), bf16[512,1536]{1,0:T(8,128)(2,1)}) %all-gather.3.cloned.1.call-update) | async-done | bytes 1572880 | tf_op jit(solution)/shard_map/all_gather | solution.py:76
  90.2 1.5 bitcast_dynamic-update-slice_fusion.6
  91.7 4.9 %collective-permute-done.5 = bf16[128,192]{1,0:T(8,128)(2,1)S(1)} collective-permute-done((bf16[128,192]{1,0:T(8,128)(2,1)S(1)}, bf16[128,192]{1,0:T(8,128)(2,1)S(1)}, u32[]{:S(2)}, u32[]{:S(2)}) %collective-permute-start.5) | collective-permute-done | bytes 49184 | tf_op jit(solution)/shard_map/ppermute | solution.py:35
  97.2 1.5 bitcast_dynamic-update-slice_fusion.4
  101.5 2.2 %fusion.8 = bf16[512,1536]{1,0:T(8,128)(2,1)} fusion(bf16[512,512]{1,0:T(8,128)(2,1)S(1)} %bitcast.100, bf16[512,1536]{1,0:T(8,128)(2,1)S(1)} %copy-done.15), kind=kOutput, calls=%fused_computation.9 | convolution fusion | flops 806879232 | bytes 3670016 | tf_op jit(solution)/shard_map/sd,sf->df/dot_general | solution.py:90
  104.2 2.1 %fusion.23 = (bf16[1,8,16,2048]{3,2,0,1:T(8,128)(2,1)}, bf16[1,8,16,2048]{3,2,0,1:T(8,128)(2,1)S(1)}) fusion(bf16[2,8,16,2048]{3,2,0,1:T(8,128)(2,1)} %all-to-all-done.1), kind=kLoop, calls=%fused_computation.62 | loop fusion | bytes 2097152 | tf_op jit(solution)/shard_map/slice | solution.py:84
  107.1 1.1 fusion.11
  108.2 27.3 %all-gather.5.cloned.1.call-done = bf16[512,2048]{1,0:T(8,128)(2,1)} async-done(((bf16[128,2048]{1,0:T(8,128)(2,1)}), bf16[512,2048]{1,0:T(8,128)(2,1)}) %all-gather.5.cloned.1.call-update) | async-done | bytes 2097168 | tf_op jit(solution)/shard_map/all_gather | solution.py:89
  135.5 2.4 %fusion.9 = bf16[192,2048]{1,0:T(8,128)(2,1)S(1)} fusion(bf16[512,192]{1,0:T(8,128)(2,1)} %bitcast.31, bf16[512,2048]{1,0:T(8,128)(2,1)} %all-gather.5.cloned.1.call-done), kind=kOutput, calls=%fused_computation.11 | convolution fusion | flops 403439616 | bytes 3080192 | tf_op jit(solution)/shard_map/sf,sd->fd/dot_general | solution.py:93
  137.9 1.5 collective-permute-start.7
  139.5 1.1 convolution_convert_fusion
  141.5 2.7 %select_bitcast_fusion = bf16[1,512,1536]{2,1,0:T(8,128)(2,1)} fusion(bf16[512,1536]{1,0:T(8,128)(2,1)} %collective-permute-done.3, bf16[512,1536]{1,0:T(8,128)(2,1)} %fusion.8, pred[]{:T(512)S(6)} %ne.47), kind=kLoop, calls=%fused_computation.21 | loop fusion | flops 786432 | bytes 4718593 | tf_op jit(solution)/shard_map/broadcast_in_dim | solution.py:111
  144.3 13.0 %collective-permute-done.7 = bf16[192,2048]{1,0:T(8,128)(2,1)S(1)} collective-permute-done((bf16[192,2048]{1,0:T(8,128)(2,1)S(1)}, bf16[192,2048]{1,0:T(8,128)(2,1)S(1)}, u32[]{:S(2)}, u32[]{:S(2)}) %collective-permute-start.7) | collective-permute-done | bytes 786464 | tf_op jit(solution)/shard_map/ppermute | solution.py:95
  (79 shorter events, 18.6 us)
Async XLA Ops:
  7.2 28.9 %copy-start = (bf16[1,768,2048]{2,1,0:T(8,128)(2,1)S(1)}, bf16[1,768,2048]{2,1,0:T(8,128)(2,1)}, u32[]{:S(2)}) copy-start(bf16[1,768,2048]{2,1,0:T(8,128)(2,1)} %param.13) | copy-start | bytes 9437188
  7.2 80.5 %all-gather.3.cloned.1.call-start = ((), (), s32[]{:S(2)}) async-start(), calls=%async_computation.2 | async-start | bytes 1966080 | tf_op jit(solution)/shard_map/all_gather | solution.py:76
  12.5 21.6 %copy-start.1 = (bf16[1,2048,1536]{2,1,0:T(8,128)(2,1)S(1)}, bf16[1,2048,1536]{2,1,0:T(8,128)(2,1)}, u32[]{:S(2)}) copy-start(bf16[1,2048,1536]{2,1,0:T(8,128)(2,1)} %param.12) | copy-start | bytes 18874372
  36.0 4.1 %copy-start.16 = (s32[8]{0:T(128)S(1)}, s32[8]{0:T(128)}, u32[]{:S(2)}) copy-start(s32[8]{0:T(128)} %param.11) | copy-start | bytes 100
  44.5 56.0 %collective-permute-start.2 = (bf16[128,512]{1,0:T(8,128)(2,1)}, bf16[128,512]{1,0:T(8,128)(2,1)}, u32[]{:S(2)}, u32[]{:S(2)}) collective-permute-start(bf16[128,512]{1,0:T(8,128)(2,1)} %get-tuple-element.16), channel_id=1, source_target_pairs={{0,3},{1,0},{2,1},{3,2},{4,7},{5,4},{6,5},{7,6},{8,11},{9,8},{10,9... | collective-permute-start | bytes 393224 | tf_op jit(solution)/shard_map/ppermute | solution.py:35
  48.1 51.5 %collective-permute-start.1 = (bf16[128,512]{1,0:T(8,128)(2,1)}, bf16[128,512]{1,0:T(8,128)(2,1)}, u32[]{:S(2)}, u32[]{:S(2)}) collective-permute-start(bf16[128,512]{1,0:T(8,128)(2,1)} %get-tuple-element.17), channel_id=1, source_target_pairs={{0,2},{1,3},{2,0},{3,1},{4,6},{5,7},{6,4},{7,5},{8,10},{9,11},{10,... | collective-permute-start | bytes 393224 | tf_op jit(solution)/shard_map/ppermute | solution.py:35
  48.1 50.5 %collective-permute-start = (bf16[128,512]{1,0:T(8,128)(2,1)}, bf16[128,512]{1,0:T(8,128)(2,1)}, u32[]{:S(2)}, u32[]{:S(2)}) collective-permute-start(bf16[128,512]{1,0:T(8,128)(2,1)} %get-tuple-element.18), channel_id=1, source_target_pairs={{0,1},{1,2},{2,3},{3,0},{4,5},{5,6},{6,7},{7,4},{8,9},{9,10},{10,1... | collective-permute-start | bytes 393224 | tf_op jit(solution)/shard_map/ppermute | solution.py:35
  49.1 4.2 %copy-start.8 = (bf16[128,768]{1,0:T(8,128)(2,1)S(1)}, bf16[128,768]{1,0:T(8,128)(2,1)}, u32[]{:S(2)}) copy-start(bf16[128,768]{1,0:T(8,128)(2,1)} %copy-done.7) | copy-start | bytes 589828
  49.9 47.2 %collective-permute-start.6 = (bf16[128,192]{1,0:T(8,128)(2,1)}, bf16[128,192]{1,0:T(8,128)(2,1)}, u32[]{:S(2)}, u32[]{:S(2)}) collective-permute-start(bf16[128,192]{1,0:T(8,128)(2,1)} %get-tuple-element.19), channel_id=1, source_target_pairs={{0,3},{1,0},{2,1},{3,2},{4,7},{5,4},{6,5},{7,6},{8,11},{9,8},{10,9... | collective-permute-start | bytes 147464 | tf_op jit(solution)/shard_map/ppermute | solution.py:35
  52.8 37.5 %collective-permute-start.4 = (bf16[128,192]{1,0:T(8,128)(2,1)}, bf16[128,192]{1,0:T(8,128)(2,1)}, u32[]{:S(2)}, u32[]{:S(2)}) collective-permute-start(bf16[128,192]{1,0:T(8,128)(2,1)} %get-tuple-element.21), channel_id=1, source_target_pairs={{0,1},{1,2},{2,3},{3,0},{4,5},{5,6},{6,7},{7,4},{8,9},{9,10},{10,1... | collective-permute-start | bytes 147464 | tf_op jit(solution)/shard_map/ppermute | solution.py:35
  59.4 30.8 %copy-start.13 = (bf16[128,192]{1,0:T(8,128)(2,1)S(1)}, bf16[128,192]{1,0:T(8,128)(2,1)}, u32[]{:S(2)}) copy-start(bf16[128,192]{1,0:T(8,128)(2,1)} %get-tuple-element.20) | copy-start | bytes 147460
  59.4 44.8 %all-to-all-start.1 = ((bf16[2,8,16,2048]{3,2,0,1:T(8,128)(2,1)}), bf16[2,8,16,2048]{3,2,0,1:T(8,128)(2,1)}, u32[]{:S(2)}, u32[]{:S(2)}) async-start(bf16[2,8,16,2048]{3,2,0,1:T(8,128)(2,1)} %pad_maximum_fusion.1), calls=%async_computation.1 | async-start | bytes 2097152 | tf_op jit(solution)/shard_map/all_to_all | solution.py:82
  63.8 71.7 %all-gather.5.cloned.1.call-start = ((), (), s32[]{:S(2)}) async-start(), calls=%async_computation.3 | async-start | bytes 2621440 | tf_op jit(solution)/shard_map/all_gather | solution.py:89
  87.7 13.7 %copy-start.15 = (bf16[512,1536]{1,0:T(8,128)(2,1)S(1)}, bf16[512,1536]{1,0:T(8,128)(2,1)}, u32[]{:S(2)}) copy-start(bf16[512,1536]{1,0:T(8,128)(2,1)} %all-gather.3.cloned.1.call-done) | copy-start | bytes 4718596
  90.2 6.4 %collective-permute-start.5 = (bf16[128,192]{1,0:T(8,128)(2,1)S(1)}, bf16[128,192]{1,0:T(8,128)(2,1)S(1)}, u32[]{:S(2)}, u32[]{:S(2)}) collective-permute-start(bf16[128,192]{1,0:T(8,128)(2,1)S(1)} %copy-done.13), channel_id=1, source_target_pairs={{0,2},{1,3},{2,0},{3,1},{4,6},{5,7},{6,4},{7,5},{8,10},{9,11},{10,... | collective-permute-start | bytes 147464 | tf_op jit(solution)/shard_map/ppermute | solution.py:35
  103.6 2.7 %copy-start.10 = (bf16[128,8,16]{0,2,1:T(8,128)(2,1)S(1)}, bf16[128,8,16]{0,2,1:T(8,128)(2,1)}, u32[]{:S(2)}) copy-start(bf16[128,8,16]{0,2,1:T(8,128)(2,1)} %select_convert_fusion) | copy-start | bytes 98308
  103.6 3.0 %copy-start.11 = (bf16[128,8,16]{0,2,1:T(8,128)(2,1)S(1)}, bf16[128,8,16]{0,2,1:T(8,128)(2,1)}, u32[]{:S(2)}) copy-start(bf16[128,8,16]{0,2,1:T(8,128)(2,1)} %get-tuple-element.23) | copy-start | bytes 98308
  103.6 37.9 %collective-permute-start.3 = (bf16[512,1536]{1,0:T(8,128)(2,1)}, bf16[512,1536]{1,0:T(8,128)(2,1)}, u32[]{:S(2)}, u32[]{:S(2)}) collective-permute-start(bf16[512,1536]{1,0:T(8,128)(2,1)} %fusion.8), channel_id=1, source_target_pairs={{0,16},{4,20},{8,24},{12,28},{16,0},{20,4},{24,8},{28,12},{1,17},{... | collective-permute-start | bytes 4718600 | tf_op jit(solution)/shard_map/ppermute | solution.py:92
  108.2 31.3 %copy-start.12 = (pred[128,8,16]{0,2,1:T(8,128)(4,1)S(1)}, pred[128,8,16]{0,2,1:T(8,128)(4,1)}, u32[]{:S(2)}) copy-start(pred[128,8,16]{0,2,1:T(8,128)(4,1)} %iota_compare_fusion) | copy-start | bytes 49156
  135.5 4.0 %copy-start.6 = (bf16[1,8,16,2048]{3,2,0,1:T(8,128)(2,1)S(1)}, bf16[1,8,16,2048]{3,2,0,1:T(8,128)(2,1)}, u32[]{:S(2)}) copy-start(bf16[1,8,16,2048]{3,2,0,1:T(8,128)(2,1)} %get-tuple-element.11) | copy-start | bytes 1572868
  135.5 5.1 %copy-start.3 = (bf16[1,8,16,2048]{3,2,0,1:T(8,128)(2,1)S(1)}, bf16[1,8,16,2048]{3,2,0,1:T(8,128)(2,1)}, u32[]{:S(2)}) copy-start(bf16[1,8,16,2048]{3,2,0,1:T(8,128)(2,1)} %copy-done.2) | copy-start | bytes 1572868
  135.5 5.1 %copy-start.5 = (bf16[128,2048]{1,0:T(8,128)(2,1)S(1)}, bf16[128,2048]{1,0:T(8,128)(2,1)}, u32[]{:S(2)}) copy-start(bf16[128,2048]{1,0:T(8,128)(2,1)} %param.8) | copy-start | bytes 1572868
  135.5 5.4 %copy-start.14 = (s32[128,8]{0,1:T(8,128)S(1)}, s32[128,8]{0,1:T(8,128)}, u32[]{:S(2)}) copy-start(s32[128,8]{0,1:T(8,128)} %param.9) | copy-start | bytes 12292
  137.9 19.3 %collective-permute-start.7 = (bf16[192,2048]{1,0:T(8,128)(2,1)S(1)}, bf16[192,2048]{1,0:T(8,128)(2,1)S(1)}, u32[]{:S(2)}, u32[]{:S(2)}) collective-permute-start(bf16[192,2048]{1,0:T(8,128)(2,1)S(1)} %fusion.9), channel_id=1, source_target_pairs={{0,16},{4,20},{8,24},{12,28},{16,0},{20,4},{24,8},{28,12},{1,17},{... | collective-permute-start | bytes 2359304 | tf_op jit(solution)/shard_map/ppermute | solution.py:95
  (4 other events, 4.2 us)
Sparse Core Ops, SparseCore 0:
  40.1 47.5 all-gather.2
  89.8 45.6 all-gather.4

commit v3 on v2

--- a/solution.py
+++ b/solution.py
@@ -74,25 +74,36 @@
     gate_up_grad = pre_grad(arrived[1], weight_out, activated, slope)
     x_slices = exchange_columns(arrived[0], group, group_count)
     all_grad = lax.all_gather(gate_up_grad, "dp", axis=0, tiled=True)
-    hidden_slices = exchange_columns(hidden, group, group_count)
     expert_out = jnp.dot(hidden, weight_out, preferred_element_type=F32).astype(BF16)
     pick_grad = jnp.einsum("sf,df->sd", gate_up_grad, weight_in, preferred_element_type=F32)
     back = jnp.stack([expert_out, pick_grad.astype(BF16)], axis=0)
     back = back.reshape(2, expert_count, capacity, model_width)
+    back, x_slices = lax.optimization_barrier((back, x_slices))
     back = lax.all_to_all(back, "expert", split_axis=1, concat_axis=1, tiled=True)
     back = back.reshape(2, slot_count, model_width)
     returned, back_grad = back[0], back[1]
 
     half = expert_count // 2
     route = [(i, (i + half) % expert_count) for i in range(expert_count)]
-    own_c, all_grad = lax.optimization_barrier((arrived[1], all_grad))
-    all_c = lax.all_gather(own_c, "dp", axis=0, tiled=True)
+    middle = model_width // 2
+    first_c, all_grad = lax.optimization_barrier((arrived[1][:, :middle], all_grad))
+    all_c1 = lax.all_gather(first_c, "dp", axis=0, tiled=True)
     grad_in = jnp.einsum("sd,sf->df", x_slices, all_grad, preferred_element_type=F32)
     grad_in = (grad_in / group_count).astype(BF16)
-    swapped_in = lax.ppermute(grad_in, "expert", route)
-    grad_out = jnp.einsum("sf,sd->fd", hidden_slices, all_c, preferred_element_type=F32)
-    grad_out = (grad_out / group_count).astype(BF16)
-    swapped_out = lax.ppermute(grad_out, "expert", route)
+    own_hidden, grad_in = lax.optimization_barrier((hidden, grad_in))
+    hidden_slices = exchange_columns(own_hidden, group, group_count)
+    half_rows = grad_in.shape[0] // 2
+    swapped_top = lax.ppermute(grad_in[:half_rows], "expert", route)
+    swapped_low = lax.ppermute(grad_in[half_rows:], "expert", route)
+    second_c, hidden_slices, all_c1, swapped_top = lax.optimization_barrier(
+        (arrived[1][:, middle:], hidden_slices, all_c1, swapped_top)
+    )
+    all_c2 = lax.all_gather(second_c, "dp", axis=0, tiled=True)
+    outs = []
+    for all_c in (all_c1, all_c2):
+        grad_out = jnp.einsum("sf,sd->fd", hidden_slices, all_c, preferred_element_type=F32)
+        grad_out = (grad_out / group_count).astype(BF16)
+        outs.append((grad_out, lax.ppermute(grad_out, "expert", route)))
 
     weigh_high = weigh.astype(BF16)
     rest = weigh - weigh_high.astype(F32)
@@ -106,8 +117,9 @@
     score_of = jnp.sum(jnp.where(slot_hot, scores, 0.0), axis=2)
     gate_grad = jnp.sum(jnp.where(pick_hot, score_of[:, None, :], 0.0), axis=2)
     x_grad = jnp.dot(select, back_grad, preferred_element_type=F32)
+    swapped_in = jnp.concatenate([swapped_top, swapped_low], axis=0)
     grad_in = jnp.where(is_moved, swapped_in, grad_in)
-    grad_out = jnp.where(is_moved, swapped_out, grad_out)
+    grad_out = jnp.concatenate([jnp.where(is_moved, theirs, own) for own, theirs in outs], axis=1)
     return (mixed.astype(BF16), x_grad.astype(BF16), gate_grad, grad_in[None], grad_out[None])
 
 

time: 166 us -> 167 us (level)
  blocking collectives: 20.6 us -> 0 us
  starting transfers between devices: 14 us -> 24.4 us
  waiting for transfers between devices: 69.1 us -> 78.2 us
  local copies, waits for them, and re-layouts: 15.4 us -> 11.9 us
  matrix products: 20.5 us -> 23.5 us
  other arithmetic: 10.4 us -> 13.1 us
    all_to_all x1 -> x0, blocking collectives: 20.6 us -> none  [shards(): lax.all_to_all(send, 'expert', split_axis=1, concat_axis=1, tiled=True)]
    all_to_all x0 -> x1, waiting for transfers between devices: none -> 13.4 us  [shards(): lax.all_to_all(send, 'expert', split_axis=1, concat_axis=1, tiled=True)]
    all_gather x1, waiting for transfers between devices: 23.9 us -> 13.9 us  [shards(): all_grad = lax.all_gather(gate_up_grad, 'dp', axis=0, tiled=True)]
    ppermute x2 -> x4, waiting for transfers between devices: 13 us -> 20.5 us  [the longest x1 15.3 us: shards(): swapped_top = lax.ppermute(grad_in[:half_rows], 'expert', route)]
    all_gather x1 -> x2, waiting for transfers between devices: 27.3 us -> 21.6 us  [the longest x1 18.8 us: shards(): all_c2 = lax.all_gather(second_c, 'dp', axis=0, tiled=True)]
    all_to_all x0 -> x1, starting transfers between devices: none -> 5.17 us  [shards(): lax.all_to_all(send, 'expert', split_axis=1, concat_axis=1, tiled=True)]
    ppermute x6, waiting for transfers between devices: 4.9 us -> 8.77 us  [exchange_columns(): lax.ppermute(piece, 'dp', [(i, (i + shift) % group_count) for i in range(...]
    dynamic_update_slice x8, local copies, waits for them, and re-layouts: 8.04 us -> 4.58 us  [exchange_columns(): whole = lax.dynamic_update_index_in_dim(whole, piece, source, axis=0)]
  transfers between devices with their start and end apart: 11 -> 15, of which waited for: 4 -> 8; matrix products, arithmetic and copies ran while one was open for 20% -> 20% of each run, Pallas kernels for 0% -> 0%
where the time goes in v3:
time: 167 us; the launch traced here: 166 us
  waiting for transfers between devices  78.2 us (47%)
  starting transfers between devices  24.4 us (15%)
  matrix products  23.5 us (14%)
  between operations  14.9 us (9%)
  other arithmetic  13.1 us (8%)
  local copies, waits for them, and re-layouts  11.9 us (7%)
    all_gather x1, waiting for transfers between devices, shards(): all_c2 = lax.all_gather(second_c, 'dp', axis=0, tiled=True)  18.8 us
    ppermute x1, waiting for transfers between devices, shards(): swapped_top = lax.ppermute(grad_in[:half_rows], 'expert', route)  15.3 us
    all_gather x1, waiting for transfers between devices, shards(): all_grad = lax.all_gather(gate_up_grad, 'dp', axis=0, tiled=True)  13.9 us
    all_to_all x1, waiting for transfers between devices, shards(): lax.all_to_all(send, 'expert', split_axis=1, concat_axis=1, tiled=True)  13.4 us
    ppermute x6, starting transfers between devices, exchange_columns(): lax.ppermute(piece, 'dp', [(i, (i + shift) % group_count) for i in range(...  9.83 us
    ppermute x6, waiting for transfers between devices, exchange_columns(): lax.ppermute(piece, 'dp', [(i, (i + shift) % group_count) for i in range(...  8.77 us
    ppermute x2, waiting for transfers between devices, shards(): outs.append((grad_out, lax.ppermute(grad_out, 'expert', route)))  5.21 us
    all_to_all x1, starting transfers between devices, shards(): lax.all_to_all(send, 'expert', split_axis=1, concat_axis=1, tiled=True)  5.17 us
  transfers between devices with their start and end apart: 15, of which 8 were waited for; matrix products, arithmetic and copies ran while one was open for 20% of the time, Pallas kernels for 0%

profile of v3, /device:TPU:0, one launch (start us, length us, event | category | flops | bytes accessed | tf_op | source)
XLA Modules:
  0.0 165.9 jit_solution(17062174777913290666)
XLA Ops:
  9.8 1.3 convolution_convert_fusion.1
  13.6 5.2 %all-to-all-start = ((bf16[2,8,16,2048]{3,2,0,1:T(8,128)(2,1)}), bf16[2,8,16,2048]{3,2,0,1:T(8,128)(2,1)}, u32[]{:S(2)}, u32[]{:S(2)}) async-start(bf16[2,8,16,2048]{3,2,0,1:T(8,128)(2,1)} %pad_maximum_fusion), calls=%async_computation | async-start | bytes 2097152 | tf_op jit(solution)/shard_map/all_to_all | solution.py:70
  20.9 13.4 %all-to-all-done = bf16[2,8,16,2048]{3,2,0,1:T(8,128)(2,1)} async-done(((bf16[2,8,16,2048]{3,2,0,1:T(8,128)(2,1)}), bf16[2,8,16,2048]{3,2,0,1:T(8,128)(2,1)}, u32[]{:S(2)}, u32[]{:S(2)}) %all-to-all-start) | async-done | bytes 1048608 | tf_op jit(solution)/shard_map/all_to_all | solution.py:70
  35.6 4.2 %fusion.2 = f32[128,1536]{1,0:T(8,128)S(1)} fusion(bf16[128,2048]{1,0:T(8,128)(2,1)S(1)} %bitcast.92, bf16[1,2048,1536]{2,1,0:T(8,128)(2,1)} %param.12), kind=kOutput, calls=%fused_computation.2 | convolution fusion | flops 805306368 | bytes 7602176 | tf_op jit(solution)/shard_map/dot_general | solution.py:11
  44.1 2.1 %collective-permute-start = (bf16[128,512]{1,0:T(8,128)(2,1)S(1)}, bf16[128,512]{1,0:T(8,128)(2,1)S(1)}, u32[]{:S(2)}, u32[]{:S(2)}) collective-permute-start(bf16[128,512]{1,0:T(8,128)(2,1)S(1)} %get-tuple-element.38), channel_id=1, source_target_pairs={{0,1},{1,2},{2,3},{3,0},{4,5},{5,6},{6,7},{7,4},{8,9},{9,10},{10,1... | collective-permute-start | bytes 393224 | tf_op jit(solution)/shard_map/ppermute | solution.py:35
  46.8 5.1 %fusion.14 = bf16[128,2048]{1,0:T(8,128)(2,1)S(1)} fusion(bf16[1,2048,1536]{2,1,0:T(8,128)(2,1)} %param.12, bf16[128,768]{1,0:T(8,128)(2,1)S(1)} %copy-done.8, bf16[128,768]{1,0:T(8,128)(2,1)S(1)} %get-tuple-element.27), kind=kOutput, calls=%fused_computation.18 | convolution fusion | flops 806354944 | bytes 7208960 | tf_op jit(solution)/shard_map/sf,df->sd/dot_general | solution.py:78
  53.9 2.5 %collective-permute-start.1 = (bf16[128,512]{1,0:T(8,128)(2,1)S(1)}, bf16[128,512]{1,0:T(8,128)(2,1)S(1)}, u32[]{:S(2)}, u32[]{:S(2)}) collective-permute-start(bf16[128,512]{1,0:T(8,128)(2,1)S(1)} %get-tuple-element.37), channel_id=1, source_target_pairs={{0,2},{1,3},{2,0},{3,1},{4,6},{5,7},{6,4},{7,5},{8,10},{9,11},{10,... | collective-permute-start | bytes 393224 | tf_op jit(solution)/shard_map/ppermute | solution.py:35
  58.6 1.6 bitcast_dynamic-update-slice_fusion.3
  60.8 7.5 %collective-permute-done.1 = bf16[128,512]{1,0:T(8,128)(2,1)S(1)} collective-permute-done((bf16[128,512]{1,0:T(8,128)(2,1)S(1)}, bf16[128,512]{1,0:T(8,128)(2,1)S(1)}, u32[]{:S(2)}, u32[]{:S(2)}) %collective-permute-start.1) | collective-permute-done | bytes 131104 | tf_op jit(solution)/shard_map/ppermute | solution.py:35
  69.7 4.2 %all-to-all-start.1 = ((bf16[2,8,16,2048]{3,2,0,1:T(8,128)(2,1)}), bf16[2,8,16,2048]{3,2,0,1:T(8,128)(2,1)}, u32[]{:S(2)}, u32[]{:S(2)}) async-start(bf16[2,8,16,2048]{3,2,0,1:T(8,128)(2,1)} %pad_maximum_fusion.1), calls=%async_computation.1 | async-start | bytes 2097152 | tf_op jit(solution)/shard_map/all_to_all | solution.py:82
  74.0 13.9 %all-gather.4.cloned.1.call-done = bf16[512,1536]{1,0:T(8,128)(2,1)} async-done(((bf16[128,1536]{1,0:T(8,128)(2,1)}), bf16[512,1536]{1,0:T(8,128)(2,1)}) %all-gather.4.cloned.1.call-update) | async-done | bytes 1572880 | tf_op jit(solution)/shard_map/all_gather | solution.py:76
  88.0 2.6 %fusion.8 = bf16[512,1536]{1,0:T(8,128)(2,1)S(1)} fusion(bf16[512,512]{1,0:T(8,128)(2,1)} %bitcast.18, bf16[512,1536]{1,0:T(8,128)(2,1)} %all-gather.4.cloned.1.call-done), kind=kOutput, calls=%fused_computation.9 | convolution fusion | flops 806879232 | bytes 3670016 | tf_op jit(solution)/shard_map/sd,sf->df/dot_general | solution.py:91
  90.8 1.6 collective-permute-start.4
  92.4 2.2 %collective-permute-start.5 = (bf16[128,192]{1,0:T(8,128)(2,1)S(1)}, bf16[128,192]{1,0:T(8,128)(2,1)S(1)}, u32[]{:S(2)}, u32[]{:S(2)}) collective-permute-start(bf16[128,192]{1,0:T(8,128)(2,1)S(1)} %get-tuple-element.39), channel_id=1, source_target_pairs={{0,3},{1,0},{2,1},{3,2},{4,7},{5,4},{6,5},{7,6},{8,11},{9,8},{10,9... | collective-permute-start | bytes 147464 | tf_op jit(solution)/shard_map/ppermute | solution.py:35
  95.6 1.4 collective-permute-start.6
  99.3 15.3 %collective-permute-done.6 = bf16[256,1536]{1,0:T(8,128)(2,1)} collective-permute-done((bf16[256,1536]{1,0:T(8,128)(2,1)S(1)}, bf16[256,1536]{1,0:T(8,128)(2,1)}, u32[]{:S(2)}, u32[]{:S(2)}) %collective-permute-start.6) | collective-permute-done | bytes 786464 | tf_op jit(solution)/shard_map/ppermute | solution.py:96
  114.6 2.7 %all-gather.6.cloned.1.call-done = bf16[512,1024]{1,0:T(8,128)(2,1)} async-done(((bf16[128,1024]{1,0:T(8,128)(2,1)}), bf16[512,1024]{1,0:T(8,128)(2,1)}) %all-gather.6.cloned.1.call-update) | async-done | bytes 1048592 | tf_op jit(solution)/shard_map/all_gather | solution.py:90
  118.7 1.4 select_reduce_fusion.1
  121.9 1.5 collective-permute-start.7
  126.8 18.8 %all-gather.8.cloned.1.call-done = bf16[512,1024]{1,0:T(8,128)(2,1)} async-done(((bf16[128,1024]{1,0:T(8,128)(2,1)}), bf16[512,1024]{1,0:T(8,128)(2,1)}) %all-gather.8.cloned.1.call-update) | async-done | bytes 1048592 | tf_op jit(solution)/shard_map/all_gather | solution.py:101
  145.6 1.6 fusion.19
  147.3 1.5 collective-permute-start.9
  148.8 3.4 %fusion.17 = bf16[1,512,1536]{2,1,0:T(8,128)(2,1)} fusion(bf16[512,1536]{1,0:T(8,128)(2,1)} %copy-done.2, bf16[256,1536]{1,0:T(8,128)(2,1)} %collective-permute-done.7, bf16[256,1536]{1,0:T(8,128)(2,1)} %collective-permute-done.6, pred[]{:T(512)S(6)} %ne.52), kind=kLoop, calls=%fused_computation.20 | loop fusion | flops 3932160 | bytes 4718593 | tf_op jit(solution)/shard_map/broadcast_in_dim | solution.py:123
  153.2 5.2 %collective-permute-done.9 = bf16[192,1024]{1,0:T(8,128)(2,1)S(1)} collective-permute-done((bf16[192,1024]{1,0:T(8,128)(2,1)S(1)}, bf16[192,1024]{1,0:T(8,128)(2,1)S(1)}, u32[]{:S(2)}, u32[]{:S(2)}) %collective-permute-start.9) | collective-permute-done | bytes 393248 | tf_op jit(solution)/shard_map/ppermute | solution.py:106
  (88 shorter events, 30.8 us)
Async XLA Ops:
  7.2 32.6 %copy-start = (bf16[1,768,2048]{2,1,0:T(8,128)(2,1)S(1)}, bf16[1,768,2048]{2,1,0:T(8,128)(2,1)}, u32[]{:S(2)}) copy-start(bf16[1,768,2048]{2,1,0:T(8,128)(2,1)} %param.13) | copy-start | bytes 9437188
  9.8 9.1 %copy-start.14 = (s32[8]{0:T(128)S(1)}, s32[8]{0:T(128)}, u32[]{:S(2)}) copy-start(s32[8]{0:T(128)} %param.11) | copy-start | bytes 100
  13.6 20.7 %all-to-all-start = ((bf16[2,8,16,2048]{3,2,0,1:T(8,128)(2,1)}), bf16[2,8,16,2048]{3,2,0,1:T(8,128)(2,1)}, u32[]{:S(2)}, u32[]{:S(2)}) async-start(bf16[2,8,16,2048]{3,2,0,1:T(8,128)(2,1)} %pad_maximum_fusion), calls=%async_computation | async-start | bytes 2097152 | tf_op jit(solution)/shard_map/all_to_all | solution.py:70
  18.7 69.1 %all-gather.4.cloned.1.call-start = ((), (), s32[]{:S(2)}) async-start(), calls=%async_computation.2 | async-start | bytes 1966080 | tf_op jit(solution)/shard_map/all_gather | solution.py:76
  35.5 4.2 %copy-start.1 = (bf16[1,8,16,2048]{3,2,0,1:T(8,128)(2,1)}, bf16[1,8,16,2048]{3,2,0,1:T(8,128)(2,1)S(1)}, u32[]{:S(2)}) copy-start(bf16[1,8,16,2048]{3,2,0,1:T(8,128)(2,1)S(1)} %get-tuple-element.31) | copy-start | bytes 1572868
  41.0 49.6 %copy-start.5 = (bf16[128,768]{1,0:T(8,128)(2,1)}, bf16[128,768]{1,0:T(8,128)(2,1)S(1)}, u32[]{:S(2)}) copy-start(bf16[128,768]{1,0:T(8,128)(2,1)S(1)} %get-tuple-element.18) | copy-start | bytes 589828
  42.5 4.4 %copy-start.8 = (bf16[128,768]{1,0:T(8,128)(2,1)S(1)}, bf16[128,768]{1,0:T(8,128)(2,1)}, u32[]{:S(2)}) copy-start(bf16[128,768]{1,0:T(8,128)(2,1)} %copy-done.7) | copy-start | bytes 589828
  44.1 16.0 %collective-permute-start = (bf16[128,512]{1,0:T(8,128)(2,1)S(1)}, bf16[128,512]{1,0:T(8,128)(2,1)S(1)}, u32[]{:S(2)}, u32[]{:S(2)}) collective-permute-start(bf16[128,512]{1,0:T(8,128)(2,1)S(1)} %get-tuple-element.38), channel_id=1, source_target_pairs={{0,1},{1,2},{2,3},{3,0},{4,5},{5,6},{6,7},{7,4},{8,9},{9,10},{10,1... | collective-permute-start | bytes 393224 | tf_op jit(solution)/shard_map/ppermute | solution.py:35
  46.8 6.2 %copy-start.4 = (bf16[1,8,16,2048]{3,2,0,1:T(8,128)(2,1)S(1)}, bf16[1,8,16,2048]{3,2,0,1:T(8,128)(2,1)}, u32[]{:S(2)}) copy-start(bf16[1,8,16,2048]{3,2,0,1:T(8,128)(2,1)} %copy-done.3) | copy-start | bytes 1572868
  53.9 14.4 %collective-permute-start.1 = (bf16[128,512]{1,0:T(8,128)(2,1)S(1)}, bf16[128,512]{1,0:T(8,128)(2,1)S(1)}, u32[]{:S(2)}, u32[]{:S(2)}) collective-permute-start(bf16[128,512]{1,0:T(8,128)(2,1)S(1)} %get-tuple-element.37), channel_id=1, source_target_pairs={{0,2},{1,3},{2,0},{3,1},{4,6},{5,7},{6,4},{7,5},{8,10},{9,11},{10,... | collective-permute-start | bytes 393224 | tf_op jit(solution)/shard_map/ppermute | solution.py:35
  56.4 12.6 %collective-permute-start.2 = (bf16[128,512]{1,0:T(8,128)(2,1)S(1)}, bf16[128,512]{1,0:T(8,128)(2,1)S(1)}, u32[]{:S(2)}, u32[]{:S(2)}) collective-permute-start(bf16[128,512]{1,0:T(8,128)(2,1)S(1)} %get-tuple-element.36), channel_id=1, source_target_pairs={{0,3},{1,0},{2,1},{3,2},{4,7},{5,4},{6,5},{7,6},{8,11},{9,8},{10,9... | collective-permute-start | bytes 393224 | tf_op jit(solution)/shard_map/ppermute | solution.py:35
  69.7 47.7 %all-to-all-start.1 = ((bf16[2,8,16,2048]{3,2,0,1:T(8,128)(2,1)}), bf16[2,8,16,2048]{3,2,0,1:T(8,128)(2,1)}, u32[]{:S(2)}, u32[]{:S(2)}) async-start(bf16[2,8,16,2048]{3,2,0,1:T(8,128)(2,1)} %pad_maximum_fusion.1), calls=%async_computation.1 | async-start | bytes 2097152 | tf_op jit(solution)/shard_map/all_to_all | solution.py:82
  73.9 43.4 %all-gather.6.cloned.1.call-start = ((), (), s32[]{:S(2)}) async-start(), calls=%async_computation.3 | async-start | bytes 1310720 | tf_op jit(solution)/shard_map/all_gather | solution.py:90
  87.9 57.7 %all-gather.8.cloned.1.call-start = ((), (), s32[]{:S(2)}) async-start(), calls=%async_computation.4 | async-start | bytes 1310720 | tf_op jit(solution)/shard_map/all_gather | solution.py:101
  90.7 7.3 %collective-permute-start.3 = (bf16[128,192]{1,0:T(8,128)(2,1)S(1)}, bf16[128,192]{1,0:T(8,128)(2,1)S(1)}, u32[]{:S(2)}, u32[]{:S(2)}) collective-permute-start(bf16[128,192]{1,0:T(8,128)(2,1)S(1)} %get-tuple-element.41), channel_id=1, source_target_pairs={{0,1},{1,2},{2,3},{3,0},{4,5},{5,6},{6,7},{7,4},{8,9},{9,10},{10,1... | collective-permute-start | bytes 147464 | tf_op jit(solution)/shard_map/ppermute | solution.py:35
  90.8 8.5 %collective-permute-start.4 = (bf16[128,192]{1,0:T(8,128)(2,1)S(1)}, bf16[128,192]{1,0:T(8,128)(2,1)S(1)}, u32[]{:S(2)}, u32[]{:S(2)}) collective-permute-start(bf16[128,192]{1,0:T(8,128)(2,1)S(1)} %get-tuple-element.40), channel_id=1, source_target_pairs={{0,2},{1,3},{2,0},{3,1},{4,6},{5,7},{6,4},{7,5},{8,10},{9,11},{10,... | collective-permute-start | bytes 147464 | tf_op jit(solution)/shard_map/ppermute | solution.py:35
  92.4 27.6 %copy-start.10 = (bf16[128,8,16]{0,2,1:T(8,128)(2,1)S(1)}, bf16[128,8,16]{0,2,1:T(8,128)(2,1)}, u32[]{:S(2)}) copy-start(bf16[128,8,16]{0,2,1:T(8,128)(2,1)} %select_convert_fusion) | copy-start | bytes 98308
  92.4 6.9 %collective-permute-start.5 = (bf16[128,192]{1,0:T(8,128)(2,1)S(1)}, bf16[128,192]{1,0:T(8,128)(2,1)S(1)}, u32[]{:S(2)}, u32[]{:S(2)}) collective-permute-start(bf16[128,192]{1,0:T(8,128)(2,1)S(1)} %get-tuple-element.39), channel_id=1, source_target_pairs={{0,3},{1,0},{2,1},{3,2},{4,7},{5,4},{6,5},{7,6},{8,11},{9,8},{10,9... | collective-permute-start | bytes 147464 | tf_op jit(solution)/shard_map/ppermute | solution.py:35
  95.6 24.8 %copy-start.11 = (bf16[128,8,16]{0,2,1:T(8,128)(2,1)S(1)}, bf16[128,8,16]{0,2,1:T(8,128)(2,1)}, u32[]{:S(2)}) copy-start(bf16[128,8,16]{0,2,1:T(8,128)(2,1)} %get-tuple-element.43) | copy-start | bytes 98308
  95.6 19.0 %collective-permute-start.6 = (bf16[256,1536]{1,0:T(8,128)(2,1)S(1)}, bf16[256,1536]{1,0:T(8,128)(2,1)}, u32[]{:S(2)}, u32[]{:S(2)}) collective-permute-start(bf16[256,1536]{1,0:T(8,128)(2,1)S(1)} %get-tuple-element.25), channel_id=1, source_target_pairs={{0,16},{4,20},{8,24},{12,28},{16,0},{20,4},{24,8},{28,12},{1,17},{... | collective-permute-start | bytes 2359304 | tf_op jit(solution)/shard_map/ppermute | solution.py:96
  120.4 4.7 %copy-start.6 = (bf16[512,1024]{1,0:T(8,128)(2,1)S(1)}, bf16[512,1024]{1,0:T(8,128)(2,1)}, u32[]{:S(2)}) copy-start(bf16[512,1024]{1,0:T(8,128)(2,1)} %all-gather.6.cloned.1.call-done) | copy-start | bytes 3145732
  121.9 26.9 %collective-permute-start.7 = (bf16[256,1536]{1,0:T(8,128)(2,1)}, bf16[256,1536]{1,0:T(8,128)(2,1)}, u32[]{:S(2)}, u32[]{:S(2)}) collective-permute-start(bf16[256,1536]{1,0:T(8,128)(2,1)} %get-tuple-element.26), channel_id=1, source_target_pairs={{0,16},{4,20},{8,24},{12,28},{16,0},{20,4},{24,8},{28,12},{1,17},{... | collective-permute-start | bytes 2359304 | tf_op jit(solution)/shard_map/ppermute | solution.py:97
  126.2 25.9 %collective-permute-start.8 = (bf16[192,1024]{1,0:T(8,128)(2,1)}, bf16[192,1024]{1,0:T(8,128)(2,1)}, u32[]{:S(2)}, u32[]{:S(2)}) collective-permute-start(bf16[192,1024]{1,0:T(8,128)(2,1)} %fusion.18), channel_id=1, source_target_pairs={{0,16},{4,20},{8,24},{12,28},{16,0},{20,4},{24,8},{28,12},{1,17},{... | collective-permute-start | bytes 1179656 | tf_op jit(solution)/shard_map/ppermute | solution.py:106
  147.3 11.2 %collective-permute-start.9 = (bf16[192,1024]{1,0:T(8,128)(2,1)S(1)}, bf16[192,1024]{1,0:T(8,128)(2,1)S(1)}, u32[]{:S(2)}, u32[]{:S(2)}) collective-permute-start(bf16[192,1024]{1,0:T(8,128)(2,1)S(1)} %fusion.19), channel_id=1, source_target_pairs={{0,16},{4,20},{8,24},{12,28},{16,0},{20,4},{24,8},{28,12},{1,17},{... | collective-permute-start | bytes 1179656 | tf_op jit(solution)/shard_map/ppermute | solution.py:106
  (6 other events, 18.1 us)
Sparse Core Ops, SparseCore 0:
  42.6 45.2 all-gather.3
  89.4 27.8 all-gather.5
  118.9 26.6 all-gather.7
